TPU v7x, 128 devices: a whole 4x4x4 slice. The times are simulated.
128 devices in a mesh: ctx: 16 (over z, y_hi, core), head: 8 (over x, y_lo).
Axes of the slice: x: 4, y: 4 (y_hi: 2, y_lo: 2; y = y_hi * 2 + y_lo), z: 4, core: 2. Of those that a mesh axis runs over, the one named last changes fastest.
Arguments:
- hidden_rows: bfloat16 [16384, 5120], P(('ctx', 'head')), may hold values from -6 to 6
- norm_gain: float32 [5120], replicated, may hold values from 0.1 to 1.9
- w_query: bfloat16 [5120, 5120], P(None, 'head'), may hold values from -1 to 1
- w_key: bfloat16 [5120, 1024], P(None, 'head'), may hold values from -1 to 1
- w_value: bfloat16 [5120, 1024], P(None, 'head'), may hold values from -0.078125 to 0.078125
- w_out: bfloat16 [5120, 5120], P('head'), may hold values from -0.078125 to 0.078125
- ancestors: int32 [128, 4], P('ctx'), may hold values from -1 to 126, as said below
Outputs:
- attention_out: bfloat16 [16384, 5120], P(('ctx', 'head'))
Inputs may be any that keep to these rules, and one draw needn't show every extreme that they name: `ancestors`: row b lists distinct earlier blocks of the same packed tree as global block numbers, nearest first, then -1 in the remaining slots (entry k + 1 is -1 wherever entry k is); every listed block lies at most 4 * (9) blocks before block b.
All inputs are finite; a program needn't handle non-finite values.
Results may differ from a plain program's by a relative error of at most 0.02.
Values may be sent and summed in bfloat16 or wider, within the bound.
A program may use at most 128 MiB of HBM per device.

v0:
```python
import jax
import jax.numpy as jnp
from jax import lax
from jax.sharding import PartitionSpec as P

HDIM = 128
BLOCK = 128
MAXA = 4


rope_base = 1000000.0


def passed_along(block, axis, distance):
    devices = range(lax.axis_size(axis))
    route = [(i - distance, i) for i in devices if i - distance in devices]
    return lax.ppermute(block, axis, route)


def rotate(tensor, position):
    half_width = tensor.shape[-1] // 2
    frequency = jnp.power(
        rope_base, -2.0 * jnp.arange(half_width, dtype=jnp.float32) / tensor.shape[-1]
    )
    angles = position[:, None] * frequency[None, :]
    cosine = jnp.cos(angles)[:, None, :]
    sine_part = jnp.sin(angles)[:, None, :]
    first_half = tensor[..., :half_width]
    second = tensor[..., half_width:]
    return jnp.concatenate(
        [first_half * cosine - second * sine_part, second * cosine + first_half * sine_part],
        axis=-1,
    )


def attend(queries, key_diag, value_diag, key_far, value_far, valid):
    blocks, length, groups, per_group, head_depth = queries.shape
    all_keys = jnp.concatenate([key_diag, key_far], axis=1)
    all_values = jnp.concatenate([value_diag, value_far], axis=1)
    scores = jnp.einsum(
        "blgpe,bkge->bgplk", queries, all_keys, precision=lax.Precision.HIGHEST
    ) * head_depth ** (-0.5)
    causal = lax.broadcasted_iota(jnp.int32, (length, length), 0) >= lax.broadcasted_iota(
        jnp.int32, (length, length), 1
    )
    far_ok = jnp.repeat(valid, length, axis=1)
    allowed = jnp.concatenate(
        [
            jnp.broadcast_to(causal[None], (blocks, length, length)),
            jnp.broadcast_to(far_ok[:, None, :], (blocks, length, far_ok.shape[1])),
        ],
        axis=2,
    )
    allowed = allowed[:, None, None, :, :]
    scores = jnp.where(allowed, scores, -1e30)
    row_max = jnp.max(scores, axis=-1, keepdims=True)
    weights = jnp.where(allowed, jnp.exp(scores - row_max), 0.0)
    row_total = jnp.sum(weights, axis=-1)
    mixture = jnp.einsum("bgplk,bkge->blgpe", weights, all_values, precision=lax.Precision.HIGHEST)
    return mixture / jnp.transpose(row_total, (0, 3, 1, 2))[..., None]


def on_device(hidden_rows, norm_gain, w_query, w_key, w_value, w_out, ancestors):
    as_float = hidden_rows.astype(jnp.float32)
    normed = (
        as_float
        * lax.rsqrt(jnp.mean(as_float * as_float, axis=1, keepdims=True) + 1e-06)
        * norm_gain
    ).astype(jnp.bfloat16)
    q_cols = w_query.shape[1]
    kv_cols = w_key.shape[1]
    row_piece = lax.all_gather(normed, "head", axis=0, tiled=True)
    projected = jnp.concatenate(
        [
            jnp.dot(row_piece, w_query, preferred_element_type=jnp.float32),
            jnp.dot(row_piece, w_key, preferred_element_type=jnp.float32),
            jnp.dot(row_piece, w_value, preferred_element_type=jnp.float32),
        ],
        axis=1,
    )
    tokens = projected.shape[0]
    shard_index = lax.axis_index("ctx")
    shard_count = lax.axis_size("ctx")
    position = (shard_index * tokens + jnp.arange(tokens, dtype=jnp.int32)).astype(jnp.float32)
    local_heads = q_cols // HDIM
    local_kv = kv_cols // HDIM
    queries = rotate(projected[:, :q_cols].reshape(tokens, local_heads, HDIM), position)
    key_rows = rotate(
        projected[:, q_cols : q_cols + kv_cols].reshape(tokens, local_kv, HDIM), position
    ).reshape(tokens, kv_cols)
    value_rows = projected[:, q_cols + kv_cols :]
    blocks = tokens // BLOCK
    block_owner = ancestors // blocks
    block_slot = (ancestors % blocks).reshape(-1)

    def collect(buffer_pair, passing, source):
        matches = (block_owner == source)[:, :, None, None]
        key_pick = jnp.take(passing[0].reshape(blocks, BLOCK, kv_cols), block_slot, axis=0).reshape(
            blocks, MAXA, BLOCK, kv_cols
        )
        value_pick = jnp.take(
            passing[1].reshape(blocks, BLOCK, kv_cols), block_slot, axis=0
        ).reshape(blocks, MAXA, BLOCK, kv_cols)
        return (
            jnp.where(matches, key_pick, buffer_pair[0]),
            jnp.where(matches, value_pick, buffer_pair[1]),
        )

    zero_buffer = jnp.zeros((blocks, MAXA, BLOCK, kv_cols), jnp.float32)
    passing = jnp.stack([key_rows, value_rows])
    gathered = collect((zero_buffer, zero_buffer), passing, shard_index)
    turn_count = shard_count - 1

    def advance(turn_step, state_pair):
        moving, buffer_pair = state_pair
        moving = passed_along(moving.astype(jnp.bfloat16), "ctx", 1).astype(moving.dtype)
        source = (shard_index - turn_step) % shard_count
        return (moving, collect(buffer_pair, moving, source))

    moved_last, gathered = lax.fori_loop(1, turn_count + 1, advance, (passing, gathered))
    per_group = local_heads // local_kv
    far_keys = gathered[0].reshape(blocks, MAXA * BLOCK, local_kv, HDIM)
    far_values = gathered[1].reshape(blocks, MAXA * BLOCK, local_kv, HDIM)
    mixture = attend(
        queries.reshape(blocks, BLOCK, local_kv, per_group, HDIM),
        key_rows.reshape(blocks, BLOCK, local_kv, HDIM),
        value_rows.reshape(blocks, BLOCK, local_kv, HDIM),
        far_keys,
        far_values,
        ancestors >= 0,
    )
    attended = mixture.reshape(tokens, q_cols).astype(jnp.bfloat16)
    summed = lax.psum_scatter(
        jnp.dot(attended, w_out, preferred_element_type=jnp.float32).astype(jnp.bfloat16),
        "head",
        scatter_dimension=0,
        tiled=True,
    )
    return summed


def solution(mesh):
    placed = (
        P(("ctx", "head"), None),
        P(),
        P(None, "head"),
        P(None, "head"),
        P(None, "head"),
        P("head", None),
        P("ctx", None),
    )
    return jax.shard_map(
        on_device, mesh=mesh, in_specs=placed, out_specs=P(("ctx", "head"), None), check_vma=False
    )
```

profile of v0, /device:TPU:104, one launch (start us, length us, event | category | flops | bytes accessed | tf_op | source)
XLA Modules:
  0.0 906.0 jit_solution(10012198710515167160)
XLA Ops:
  8.3 2.8 fusion.11
  13.3 3.1 multiply_cosine_fusion
  16.4 202.8 %all-gather.2.cloned.1.call-done = bf16[1024,5120]{1,0:T(8,128)(2,1)} async-done(((bf16[128,5120]{1,0:T(8,128)(2,1)}), bf16[1024,5120]{1,0:T(8,128)(2,1)}) %all-gather.2.cloned.1.call-update) | async-done | bytes 10485776 | tf_op jit(solution)/shard_map/all_gather | solution.py:72
  219.2 6.6 convolution_bitcast_fusion
  225.9 2.3 fusion.27
  229.4 2.9 fusion.37
  233.3 11.6 %fusion.38 = f32[1024,640]{0,1:T(8,128)S(1)} fusion(bf16[1024,5120]{1,0:T(8,128)(2,1)} %all-gather.2.cloned.1.call-done, bf16[5120,640]{1,0:T(8,128)(2,1)} %param.13), kind=kOutput, calls=%fused_computation.88 | convolution fusion | flops 6710886400 | bytes 19660800 | tf_op jit(solution)/shard_map/dot_general | solution.py:75
  249.0 2.0 gather_fusion.3
  251.9 2.2 broadcast_select_fusion.4
  254.1 2.5 broadcast_select_fusion.6
  256.6 372.4 %while.19 = (s32[]{:T(128)}, bf16[2,1024,128]{2,1,0:T(8,128)(2,1)}, f32[8,4,128,128]{3,2,1,0:T(8,128)}, f32[8,4,128,128]{3,2,1,0:T(8,128)}, s32[]{:T(128)}, /*in...) while((s32[]{:T(128)}, bf16[2,1024,128]{2,1,0:T(8,128)(2,1)}, ...), condition=%wide.region_2.4_spmd, body=%wide.region_1.3_spmd.sunk | while | flops 2098510 | bytes 38802756 | solution.py:120
  259.1 11.1 %collective-permute-done = bf16[2,1024,128]{2,1,0:T(8,128)(2,1)S(1)} collective-permute-done((bf16[2,1024,128]{2,1,0:T(8,128)(2,1)}, bf16[2,1024,128]{2,1,0:T(8,128)(2,1)S(1)}, u32[]{:S(2)}, u32[]{:S(2)}) %collective-permute-start) | collective-permute-done | bytes 524320 | tf_op jit(solution)/shard_map/while/body/eval_jaxpr/ppermute | solution.py:17
  273.7 2.1 broadcast_select_fusion.10
  275.9 5.2 broadcast_select_fusion.11
  283.9 11.1 %collective-permute-done = bf16[2,1024,128]{2,1,0:T(8,128)(2,1)S(1)} collective-permute-done((bf16[2,1024,128]{2,1,0:T(8,128)(2,1)}, bf16[2,1024,128]{2,1,0:T(8,128)(2,1)S(1)}, u32[]{:S(2)}, u32[]{:S(2)}) %collective-permute-start) | collective-permute-done | bytes 524320 | tf_op jit(solution)/shard_map/while/body/eval_jaxpr/ppermute | solution.py:17
  298.5 2.1 broadcast_select_fusion.10
  300.7 5.2 broadcast_select_fusion.11
  308.7 11.1 %collective-permute-done = bf16[2,1024,128]{2,1,0:T(8,128)(2,1)S(1)} collective-permute-done((bf16[2,1024,128]{2,1,0:T(8,128)(2,1)}, bf16[2,1024,128]{2,1,0:T(8,128)(2,1)S(1)}, u32[]{:S(2)}, u32[]{:S(2)}) %collective-permute-start) | collective-permute-done | bytes 524320 | tf_op jit(solution)/shard_map/while/body/eval_jaxpr/ppermute | solution.py:17
  323.3 2.1 broadcast_select_fusion.10
  325.5 5.2 broadcast_select_fusion.11
  333.5 11.1 %collective-permute-done = bf16[2,1024,128]{2,1,0:T(8,128)(2,1)S(1)} collective-permute-done((bf16[2,1024,128]{2,1,0:T(8,128)(2,1)}, bf16[2,1024,128]{2,1,0:T(8,128)(2,1)S(1)}, u32[]{:S(2)}, u32[]{:S(2)}) %collective-permute-start) | collective-permute-done | bytes 524320 | tf_op jit(solution)/shard_map/while/body/eval_jaxpr/ppermute | solution.py:17
  348.1 2.1 broadcast_select_fusion.10
  350.3 5.2 broadcast_select_fusion.11
  358.3 11.1 %collective-permute-done = bf16[2,1024,128]{2,1,0:T(8,128)(2,1)S(1)} collective-permute-done((bf16[2,1024,128]{2,1,0:T(8,128)(2,1)}, bf16[2,1024,128]{2,1,0:T(8,128)(2,1)S(1)}, u32[]{:S(2)}, u32[]{:S(2)}) %collective-permute-start) | collective-permute-done | bytes 524320 | tf_op jit(solution)/shard_map/while/body/eval_jaxpr/ppermute | solution.py:17
  372.9 2.1 broadcast_select_fusion.10
  375.0 5.2 broadcast_select_fusion.11
  383.1 11.1 %collective-permute-done = bf16[2,1024,128]{2,1,0:T(8,128)(2,1)S(1)} collective-permute-done((bf16[2,1024,128]{2,1,0:T(8,128)(2,1)}, bf16[2,1024,128]{2,1,0:T(8,128)(2,1)S(1)}, u32[]{:S(2)}, u32[]{:S(2)}) %collective-permute-start) | collective-permute-done | bytes 524320 | tf_op jit(solution)/shard_map/while/body/eval_jaxpr/ppermute | solution.py:17
  397.7 2.1 broadcast_select_fusion.10
  399.8 5.2 broadcast_select_fusion.11
  407.9 11.1 %collective-permute-done = bf16[2,1024,128]{2,1,0:T(8,128)(2,1)S(1)} collective-permute-done((bf16[2,1024,128]{2,1,0:T(8,128)(2,1)}, bf16[2,1024,128]{2,1,0:T(8,128)(2,1)S(1)}, u32[]{:S(2)}, u32[]{:S(2)}) %collective-permute-start) | collective-permute-done | bytes 524320 | tf_op jit(solution)/shard_map/while/body/eval_jaxpr/ppermute | solution.py:17
  422.5 2.1 broadcast_select_fusion.10
  424.6 5.2 broadcast_select_fusion.11
  432.7 11.1 %collective-permute-done = bf16[2,1024,128]{2,1,0:T(8,128)(2,1)S(1)} collective-permute-done((bf16[2,1024,128]{2,1,0:T(8,128)(2,1)}, bf16[2,1024,128]{2,1,0:T(8,128)(2,1)S(1)}, u32[]{:S(2)}, u32[]{:S(2)}) %collective-permute-start) | collective-permute-done | bytes 524320 | tf_op jit(solution)/shard_map/while/body/eval_jaxpr/ppermute | solution.py:17
  447.3 2.1 broadcast_select_fusion.10
  449.4 5.2 broadcast_select_fusion.11
  457.5 11.1 %collective-permute-done = bf16[2,1024,128]{2,1,0:T(8,128)(2,1)S(1)} collective-permute-done((bf16[2,1024,128]{2,1,0:T(8,128)(2,1)}, bf16[2,1024,128]{2,1,0:T(8,128)(2,1)S(1)}, u32[]{:S(2)}, u32[]{:S(2)}) %collective-permute-start) | collective-permute-done | bytes 524320 | tf_op jit(solution)/shard_map/while/body/eval_jaxpr/ppermute | solution.py:17
  472.1 2.1 broadcast_select_fusion.10
  474.2 5.2 broadcast_select_fusion.11
  482.3 11.1 %collective-permute-done = bf16[2,1024,128]{2,1,0:T(8,128)(2,1)S(1)} collective-permute-done((bf16[2,1024,128]{2,1,0:T(8,128)(2,1)}, bf16[2,1024,128]{2,1,0:T(8,128)(2,1)S(1)}, u32[]{:S(2)}, u32[]{:S(2)}) %collective-permute-start) | collective-permute-done | bytes 524320 | tf_op jit(solution)/shard_map/while/body/eval_jaxpr/ppermute | solution.py:17
  496.9 2.1 broadcast_select_fusion.10
  499.0 5.2 broadcast_select_fusion.11
  507.1 11.1 %collective-permute-done = bf16[2,1024,128]{2,1,0:T(8,128)(2,1)S(1)} collective-permute-done((bf16[2,1024,128]{2,1,0:T(8,128)(2,1)}, bf16[2,1024,128]{2,1,0:T(8,128)(2,1)S(1)}, u32[]{:S(2)}, u32[]{:S(2)}) %collective-permute-start) | collective-permute-done | bytes 524320 | tf_op jit(solution)/shard_map/while/body/eval_jaxpr/ppermute | solution.py:17
  521.7 2.1 broadcast_select_fusion.10
  523.8 5.2 broadcast_select_fusion.11
  531.8 11.1 %collective-permute-done = bf16[2,1024,128]{2,1,0:T(8,128)(2,1)S(1)} collective-permute-done((bf16[2,1024,128]{2,1,0:T(8,128)(2,1)}, bf16[2,1024,128]{2,1,0:T(8,128)(2,1)S(1)}, u32[]{:S(2)}, u32[]{:S(2)}) %collective-permute-start) | collective-permute-done | bytes 524320 | tf_op jit(solution)/shard_map/while/body/eval_jaxpr/ppermute | solution.py:17
  546.5 2.1 broadcast_select_fusion.10
  548.6 5.2 broadcast_select_fusion.11
  556.6 11.1 %collective-permute-done = bf16[2,1024,128]{2,1,0:T(8,128)(2,1)S(1)} collective-permute-done((bf16[2,1024,128]{2,1,0:T(8,128)(2,1)}, bf16[2,1024,128]{2,1,0:T(8,128)(2,1)S(1)}, u32[]{:S(2)}, u32[]{:S(2)}) %collective-permute-start) | collective-permute-done | bytes 524320 | tf_op jit(solution)/shard_map/while/body/eval_jaxpr/ppermute | solution.py:17
  571.3 2.1 broadcast_select_fusion.10
  573.4 5.2 broadcast_select_fusion.11
  581.4 11.1 %collective-permute-done = bf16[2,1024,128]{2,1,0:T(8,128)(2,1)S(1)} collective-permute-done((bf16[2,1024,128]{2,1,0:T(8,128)(2,1)}, bf16[2,1024,128]{2,1,0:T(8,128)(2,1)S(1)}, u32[]{:S(2)}, u32[]{:S(2)}) %collective-permute-start) | collective-permute-done | bytes 524320 | tf_op jit(solution)/shard_map/while/body/eval_jaxpr/ppermute | solution.py:17
  596.1 2.1 broadcast_select_fusion.10
  598.2 5.2 broadcast_select_fusion.11
  606.2 11.1 %collective-permute-done = bf16[2,1024,128]{2,1,0:T(8,128)(2,1)S(1)} collective-permute-done((bf16[2,1024,128]{2,1,0:T(8,128)(2,1)}, bf16[2,1024,128]{2,1,0:T(8,128)(2,1)S(1)}, u32[]{:S(2)}, u32[]{:S(2)}) %collective-permute-start) | collective-permute-done | bytes 524320 | tf_op jit(solution)/shard_map/while/body/eval_jaxpr/ppermute | solution.py:17
  620.9 2.1 broadcast_select_fusion.10
  623.0 5.2 broadcast_select_fusion.11
  629.0 3.0 copy.47
  632.0 2.1 copy.48
  634.1 3.1 multiply_subtract_fusion
  638.5 16.1 %fusion.2 = (f32[8,5,128]{2,1,0:T(8,128)S(1)}, f32[8,640,128,5]{2,1,3,0:T(8,128)}) fusion(pred[8,128,640]{1,2,0:T(8,128)(4,1)S(1)} %copy-done.6, f32[8,128,5,128]{3,1,0,2:T(8,128)S(1)} %bitcast.94, f32[8,512,1,128]{3,1,0,2:T(8,128)} %bitcast.18, f32[8,128,1,128]{3,1,0,2:T(8,128)S(1)} %bitcast.96), kind=kOutput, calls=%fused_computation.16 | convolution fusion | flops 5043645440 | bytes 19025920 | tf_op jit(solution)/shard_map/blgpe,bkge->bgplk/dot_general | solution.py:40
  654.6 8.2 fusion.3
  662.9 15.0 %fusion.17 = bf16[8,128,1,5,128]{1,4,3,0,2:T(8,128)(2,1)S(1)} fusion(f32[8,640,128,5]{2,1,3,0:T(8,128)} %get-tuple-element.229, f32[8,5,128]{2,1,0:T(8,128)S(1)} %get-tuple-element.228, pred[8,128,640]{1,2,0:T(8,128)(4,1)S(1)} %copy-done.6, f32[8,512,1,128]{1,3,0,2:T(8,128)S(1)} %copy-done.11, f32[8,128,1,128]{1,3,0,2:T(8,128)S(1)} %copy-done.12, ...), kind=kOutput, calls=%fused_computation.38 | convolution fusion | flops 5048238080 | bytes 17735680 | tf_op jit(solution)/shard_map/bgplk,bkge->blgpe/dot_general | solution.py:59
  678.8 11.2 %convolution_convert_fusion = bf16[1024,5120]{1,0:T(8,128)(2,1)} fusion(bf16[640,5120]{1,0:T(8,128)(2,1)S(1)} %bitcast.106, bf16[80,8,8,128]{3,2,1,0:T(8,128)(2,1)S(1)} %bitcast.103), kind=kOutput, calls=%fused_computation.17 | convolution fusion | flops 6716129280 | bytes 18350080 | tf_op jit(solution)/shard_map/dot_general | solution.py:134
  690.0 208.9 %reduce-scatter.2.cloned.1.call-done = bf16[128,5120]{1,0:T(8,128)(2,1)} async-done(((bf16[1024,5120]{1,0:T(8,128)(2,1)}), bf16[128,5120]{1,0:T(8,128)(2,1)}) %reduce-scatter.2.cloned.1.call-update) | async-done | bytes 1310736 | tf_op jit(solution)/shard_map/reduce_scatter | solution.py:133
  (259 shorter events, 107.9 us)
Async XLA Ops:
  6.5 212.7 %copy-start = (bf16[5120,128]{1,0:T(8,128)(2,1)S(1)}, bf16[5120,128]{1,0:T(8,128)(2,1)}, u32[]{:S(2)}) copy-start(bf16[5120,128]{1,0:T(8,128)(2,1)} %param.14) | copy-start | bytes 3932164
  6.5 4.6 copy-start.13
  6.5 212.7 %all-gather.2.cloned.1.call-start = ((), (), s32[]{:S(2)}) async-start(), calls=%async_computation.1 | async-start | bytes 11796480 | tf_op jit(solution)/shard_map/all_gather | solution.py:72
  11.1 887.8 %reduce-scatter.2.cloned.1.call-start = ((), (), s32[]{:S(2)}) async-start(), calls=%async_computation.2 | async-start | bytes 11796480 | tf_op jit(solution)/shard_map/reduce_scatter | solution.py:133
  219.2 10.2 %copy-start.14 = (bf16[1024,5120]{1,0:T(8,128)(2,1)S(1)}, bf16[1024,5120]{1,0:T(8,128)(2,1)}, u32[]{:S(2)}) copy-start(bf16[1024,5120]{1,0:T(8,128)(2,1)} %all-gather.2.cloned.1.call-done) | copy-start | bytes 31457284
  225.9 3.5 copy-start.15
  228.3 19.9 %copy-start.4 = (f32[1024,1,128]{2,0,1:T(8,128)}, f32[1024,1,128]{2,0,1:T(8,128)S(1)}, u32[]{:S(2)}) copy-start(f32[1024,1,128]{2,0,1:T(8,128)S(1)} %pad_maximum_fusion.2) | copy-start | bytes 1572868
  248.9 2.1 copy-start.8
  257.1 13.1 %collective-permute-start = (bf16[2,1024,128]{2,1,0:T(8,128)(2,1)}, bf16[2,1024,128]{2,1,0:T(8,128)(2,1)S(1)}, u32[]{:S(2)}, u32[]{:S(2)}) collective-permute-start(bf16[2,1024,128]{2,1,0:T(8,128)(2,1)} %get-tuple-element.297), channel_id=1, source_target_pairs={{0,8},{8,16},{16,24},{24,32},{32,40},{40,48},{48,56},{56,64},{64,7... | collective-permute-start | bytes 1572872 | tf_op jit(solution)/shard_map/while/body/eval_jaxpr/ppermute | solution.py:17
  270.2 0.8 copy-start.2
  275.8 5.2 copy-start.3
  281.9 13.1 %collective-permute-start = (bf16[2,1024,128]{2,1,0:T(8,128)(2,1)}, bf16[2,1024,128]{2,1,0:T(8,128)(2,1)S(1)}, u32[]{:S(2)}, u32[]{:S(2)}) collective-permute-start(bf16[2,1024,128]{2,1,0:T(8,128)(2,1)} %get-tuple-element.297), channel_id=1, source_target_pairs={{0,8},{8,16},{16,24},{24,32},{32,40},{40,48},{48,56},{56,64},{64,7... | collective-permute-start | bytes 1572872 | tf_op jit(solution)/shard_map/while/body/eval_jaxpr/ppermute | solution.py:17
  295.0 0.8 copy-start.2
  300.6 5.2 copy-start.3
  306.7 13.1 %collective-permute-start = (bf16[2,1024,128]{2,1,0:T(8,128)(2,1)}, bf16[2,1024,128]{2,1,0:T(8,128)(2,1)S(1)}, u32[]{:S(2)}, u32[]{:S(2)}) collective-permute-start(bf16[2,1024,128]{2,1,0:T(8,128)(2,1)} %get-tuple-element.297), channel_id=1, source_target_pairs={{0,8},{8,16},{16,24},{24,32},{32,40},{40,48},{48,56},{56,64},{64,7... | collective-permute-start | bytes 1572872 | tf_op jit(solution)/shard_map/while/body/eval_jaxpr/ppermute | solution.py:17
  319.8 0.8 copy-start.2
  325.4 5.2 copy-start.3
  331.5 13.1 %collective-permute-start = (bf16[2,1024,128]{2,1,0:T(8,128)(2,1)}, bf16[2,1024,128]{2,1,0:T(8,128)(2,1)S(1)}, u32[]{:S(2)}, u32[]{:S(2)}) collective-permute-start(bf16[2,1024,128]{2,1,0:T(8,128)(2,1)} %get-tuple-element.297), channel_id=1, source_target_pairs={{0,8},{8,16},{16,24},{24,32},{32,40},{40,48},{48,56},{56,64},{64,7... | collective-permute-start | bytes 1572872 | tf_op jit(solution)/shard_map/while/body/eval_jaxpr/ppermute | solution.py:17
  344.6 0.8 copy-start.2
  350.2 5.2 copy-start.3
  356.3 13.1 %collective-permute-start = (bf16[2,1024,128]{2,1,0:T(8,128)(2,1)}, bf16[2,1024,128]{2,1,0:T(8,128)(2,1)S(1)}, u32[]{:S(2)}, u32[]{:S(2)}) collective-permute-start(bf16[2,1024,128]{2,1,0:T(8,128)(2,1)} %get-tuple-element.297), channel_id=1, source_target_pairs={{0,8},{8,16},{16,24},{24,32},{32,40},{40,48},{48,56},{56,64},{64,7... | collective-permute-start | bytes 1572872 | tf_op jit(solution)/shard_map/while/body/eval_jaxpr/ppermute | solution.py:17
  369.4 0.8 copy-start.2
  375.0 5.2 copy-start.3
  381.1 13.1 %collective-permute-start = (bf16[2,1024,128]{2,1,0:T(8,128)(2,1)}, bf16[2,1024,128]{2,1,0:T(8,128)(2,1)S(1)}, u32[]{:S(2)}, u32[]{:S(2)}) collective-permute-start(bf16[2,1024,128]{2,1,0:T(8,128)(2,1)} %get-tuple-element.297), channel_id=1, source_target_pairs={{0,8},{8,16},{16,24},{24,32},{32,40},{40,48},{48,56},{56,64},{64,7... | collective-permute-start | bytes 1572872 | tf_op jit(solution)/shard_map/while/body/eval_jaxpr/ppermute | solution.py:17
  394.2 0.8 copy-start.2
  399.8 5.2 copy-start.3
  405.9 13.1 %collective-permute-start = (bf16[2,1024,128]{2,1,0:T(8,128)(2,1)}, bf16[2,1024,128]{2,1,0:T(8,128)(2,1)S(1)}, u32[]{:S(2)}, u32[]{:S(2)}) collective-permute-start(bf16[2,1024,128]{2,1,0:T(8,128)(2,1)} %get-tuple-element.297), channel_id=1, source_target_pairs={{0,8},{8,16},{16,24},{24,32},{32,40},{40,48},{48,56},{56,64},{64,7... | collective-permute-start | bytes 1572872 | tf_op jit(solution)/shard_map/while/body/eval_jaxpr/ppermute | solution.py:17
  419.0 0.8 copy-start.2
  424.6 5.2 copy-start.3
  430.7 13.1 %collective-permute-start = (bf16[2,1024,128]{2,1,0:T(8,128)(2,1)}, bf16[2,1024,128]{2,1,0:T(8,128)(2,1)S(1)}, u32[]{:S(2)}, u32[]{:S(2)}) collective-permute-start(bf16[2,1024,128]{2,1,0:T(8,128)(2,1)} %get-tuple-element.297), channel_id=1, source_target_pairs={{0,8},{8,16},{16,24},{24,32},{32,40},{40,48},{48,56},{56,64},{64,7... | collective-permute-start | bytes 1572872 | tf_op jit(solution)/shard_map/while/body/eval_jaxpr/ppermute | solution.py:17
  443.8 0.8 copy-start.2
  449.4 5.2 copy-start.3
  455.5 13.1 %collective-permute-start = (bf16[2,1024,128]{2,1,0:T(8,128)(2,1)}, bf16[2,1024,128]{2,1,0:T(8,128)(2,1)S(1)}, u32[]{:S(2)}, u32[]{:S(2)}) collective-permute-start(bf16[2,1024,128]{2,1,0:T(8,128)(2,1)} %get-tuple-element.297), channel_id=1, source_target_pairs={{0,8},{8,16},{16,24},{24,32},{32,40},{40,48},{48,56},{56,64},{64,7... | collective-permute-start | bytes 1572872 | tf_op jit(solution)/shard_map/while/body/eval_jaxpr/ppermute | solution.py:17
  468.6 0.8 copy-start.2
  474.2 5.2 copy-start.3
  480.3 13.1 %collective-permute-start = (bf16[2,1024,128]{2,1,0:T(8,128)(2,1)}, bf16[2,1024,128]{2,1,0:T(8,128)(2,1)S(1)}, u32[]{:S(2)}, u32[]{:S(2)}) collective-permute-start(bf16[2,1024,128]{2,1,0:T(8,128)(2,1)} %get-tuple-element.297), channel_id=1, source_target_pairs={{0,8},{8,16},{16,24},{24,32},{32,40},{40,48},{48,56},{56,64},{64,7... | collective-permute-start | bytes 1572872 | tf_op jit(solution)/shard_map/while/body/eval_jaxpr/ppermute | solution.py:17
  493.4 0.8 copy-start.2
  499.0 5.2 copy-start.3
  505.1 13.1 %collective-permute-start = (bf16[2,1024,128]{2,1,0:T(8,128)(2,1)}, bf16[2,1024,128]{2,1,0:T(8,128)(2,1)S(1)}, u32[]{:S(2)}, u32[]{:S(2)}) collective-permute-start(bf16[2,1024,128]{2,1,0:T(8,128)(2,1)} %get-tuple-element.297), channel_id=1, source_target_pairs={{0,8},{8,16},{16,24},{24,32},{32,40},{40,48},{48,56},{56,64},{64,7... | collective-permute-start | bytes 1572872 | tf_op jit(solution)/shard_map/while/body/eval_jaxpr/ppermute | solution.py:17
  518.2 0.8 copy-start.2
  523.8 5.2 copy-start.3
  529.9 13.1 %collective-permute-start = (bf16[2,1024,128]{2,1,0:T(8,128)(2,1)}, bf16[2,1024,128]{2,1,0:T(8,128)(2,1)S(1)}, u32[]{:S(2)}, u32[]{:S(2)}) collective-permute-start(bf16[2,1024,128]{2,1,0:T(8,128)(2,1)} %get-tuple-element.297), channel_id=1, source_target_pairs={{0,8},{8,16},{16,24},{24,32},{32,40},{40,48},{48,56},{56,64},{64,7... | collective-permute-start | bytes 1572872 | tf_op jit(solution)/shard_map/while/body/eval_jaxpr/ppermute | solution.py:17
  543.0 0.8 copy-start.2
  548.6 5.2 copy-start.3
  554.6 13.1 %collective-permute-start = (bf16[2,1024,128]{2,1,0:T(8,128)(2,1)}, bf16[2,1024,128]{2,1,0:T(8,128)(2,1)S(1)}, u32[]{:S(2)}, u32[]{:S(2)}) collective-permute-start(bf16[2,1024,128]{2,1,0:T(8,128)(2,1)} %get-tuple-element.297), channel_id=1, source_target_pairs={{0,8},{8,16},{16,24},{24,32},{32,40},{40,48},{48,56},{56,64},{64,7... | collective-permute-start | bytes 1572872 | tf_op jit(solution)/shard_map/while/body/eval_jaxpr/ppermute | solution.py:17
  567.8 0.8 copy-start.2
  573.4 5.2 copy-start.3
  579.4 13.1 %collective-permute-start = (bf16[2,1024,128]{2,1,0:T(8,128)(2,1)}, bf16[2,1024,128]{2,1,0:T(8,128)(2,1)S(1)}, u32[]{:S(2)}, u32[]{:S(2)}) collective-permute-start(bf16[2,1024,128]{2,1,0:T(8,128)(2,1)} %get-tuple-element.297), channel_id=1, source_target_pairs={{0,8},{8,16},{16,24},{24,32},{32,40},{40,48},{48,56},{56,64},{64,7... | collective-permute-start | bytes 1572872 | tf_op jit(solution)/shard_map/while/body/eval_jaxpr/ppermute | solution.py:17
  592.5 0.8 copy-start.2
  598.2 5.2 copy-start.3
  604.2 13.1 %collective-permute-start = (bf16[2,1024,128]{2,1,0:T(8,128)(2,1)}, bf16[2,1024,128]{2,1,0:T(8,128)(2,1)S(1)}, u32[]{:S(2)}, u32[]{:S(2)}) collective-permute-start(bf16[2,1024,128]{2,1,0:T(8,128)(2,1)} %get-tuple-element.297), channel_id=1, source_target_pairs={{0,8},{8,16},{16,24},{24,32},{32,40},{40,48},{48,56},{56,64},{64,7... | collective-permute-start | bytes 1572872 | tf_op jit(solution)/shard_map/while/body/eval_jaxpr/ppermute | solution.py:17
  617.3 0.8 copy-start.2
  623.0 5.2 copy-start.3
  629.0 3.0 copy-start.7
  632.0 2.1 copy-start.9
  632.0 2.1 copy-start.10
  637.2 1.0 copy-start.5
  637.3 1.2 copy-start.6
  654.6 8.3 copy-start.11
  654.6 8.3 copy-start.12
  654.6 24.1 %slice-start = ((s8[6553600]{0:T(1024)(128)(4,1)}), s8[4194304]{0:T(1024)(128)(4,1)S(1)}, s32[]{:S(2)}) async-start(s8[6553600]{0:T(1024)(128)(4,1)} %bitcast.105), calls=%async_computation.3 | async-start | bytes 8388608
  662.9 15.9 %slice-start.1 = ((s8[6553600]{0:T(1024)(128)(4,1)}), s8[2359296]{0:T(1024)(128)(4,1)S(1)}, s32[]{:S(2)}) async-start(s8[6553600]{0:T(1024)(128)(4,1)} %bitcast.105), calls=%async_computation.4 | async-start | bytes 4718592
  690.0 209.0 %copy-start.1 = (bf16[5120,128]{1,0:T(8,128)(2,1)S(1)}, bf16[5120,128]{1,0:T(8,128)(2,1)}, u32[]{:S(2)}) copy-start(bf16[5120,128]{1,0:T(8,128)(2,1)} %param.14) | copy-start | bytes 3932164
Sparse Core Ops, SparseCore 0:
  11.2 207.9 all-gather.1
  690.1 208.7 reduce-scatter.1
where the time goes:
time: 919 us; the launch traced here: 906 us
  waiting for transfers between devices  578 us (63%)
  other arithmetic  139 us (15%)
  local copies, waits for them, and re-layouts  80.3 us (9%)
  matrix products  63.4 us (7%)
  starting transfers between devices  28.7 us (3%)
  between operations  13.9 us (2%)
    reduce_scatter x1, waiting for transfers between devices, on_device(): lax.psum_scatter(jnp.dot(attended, w_out, preferred_element_type=jnp.floa...  209 us
    all_gather x1, waiting for transfers between devices, on_device(): row_piece = lax.all_gather(normed, 'head', axis=0, tiled=True)  203 us
    ppermute x15, waiting for transfers between devices, passed_along(): return lax.ppermute(block, axis, route)  167 us
    select_n x16, other arithmetic, collect(): jnp.where(matches, value_pick, buffer_pair[1])  80.3 us
    select_n x16, other arithmetic, collect(): jnp.take(passing[1].reshape(blocks, BLOCK, kv_cols), block_slot, axis=0)  33.8 us
    gather x16, local copies, waits for them, and re-layouts, collect(): jnp.take(passing[1].reshape(blocks, BLOCK, kv_cols), block_slot, axis=0)  32.5 us
    ppermute x15, starting transfers between devices, passed_along(): return lax.ppermute(block, axis, route)  28.6 us
    while x75, local copies, waits for them, and re-layouts  24 us
  transfers between devices with their start and end apart: 17, of which 17 were waited for; matrix products, arithmetic and copies ran while one was open for 1% of the time, Pallas kernels for 0%

commit v1 on v0

v1 whole, which is shorter than its diff:
```python
import functools

import jax
import jax.numpy as jnp
import numpy as np
from jax import lax
from jax.experimental import pallas as pl
from jax.experimental.pallas import tpu as pltpu
from jax.sharding import PartitionSpec as P

D = 5120
HDIM = 128
BLOCK = 128
MAXA = 4
PER_GROUP = 5
QCOLS = PER_GROUP * HDIM
HALF = BLOCK // 2
ROPE_BASE = 1000000.0
Q_SCALE = float(HDIM**-0.5 * np.log2(np.e))
MESH = pl.DeviceIdType.MESH
F32 = jnp.float32
BF16 = jnp.bfloat16
N_OUT = 512


def rope_tables():
    frequency = ROPE_BASE ** (-2.0 * np.arange(HDIM // 2) / HDIM)
    frequency = np.concatenate([frequency, frequency])
    inner = np.arange(BLOCK)[:, None] * frequency[None, :]
    outer = np.arange(128)[:, None] * float(BLOCK) * frequency[None, :]
    return [f(t).astype(np.float32) for t in (inner, outer) for f in (np.cos, np.sin)]


def kernel(
    hid, gain, wq_h, wk_h, wv_h, wo_h, anc_h, ci, si, cb, sb,
    out,
    xb, wkv, wq, wo, qs, kv, att, rb, far, fin, anc_v, anc_s,
    ag_s, ag_r, ws_s, ws_r, wz_s, wl, kv_s, kv_r, rs_s, rs_r, an_s, an_r, an_l,
):
    c = lax.axis_index("ctx")
    h = lax.axis_index("head")
    x = h // 2
    par = h % 2
    yh = (c // 2) % 2
    z = c // 4
    k = c % 2
    y = yh * 2 + par
    zp = z % 2
    span = 2 * z + yh
    own = k == par

    def dev(x, y, z, k):
        return {"ctx": z * 4 + (y // 2) * 2 + k, "head": x * 2 + y % 2}

    right = dev((x + 1) % 4, y, z, k)
    left = dev((x + 3) % 4, y, z, k)
    sib = dev(x, y, z, 1 - k)

    def send(src, dst, ssem, rsem, to):
        return pltpu.make_async_remote_copy(
            src_ref=src, dst_ref=dst, send_sem=ssem, recv_sem=rsem, device_id=to, device_id_type=MESH
        )

    barrier = pltpu.get_barrier_semaphore()
    greeted = [right, left, sib]
    greeted += [dev(x, (y + d) % 4, z, k) for d in (1, 2, 3)]
    greeted += [dev(x, (y + d) % 4, z, 1 - k) for d in (1, 3)]
    greeted += [dev(x, (y + d) % 4, (z + e) % 4, k) for e in (1, 3) for d in range(4)]
    for to in greeted:
        pl.semaphore_signal(barrier, 1, device_id=to, device_id_type=MESH)

    local = [
        pltpu.make_async_copy(wk_h, wkv.at[:, pl.ds(0, HDIM)], wl.at[0]),
        pltpu.make_async_copy(wv_h, wkv.at[:, pl.ds(HDIM, HDIM)], wl.at[1]),
        pltpu.make_async_copy(wq_h, wq, wl.at[2]),
        pltpu.make_async_copy(wo_h, wo, wl.at[3]),
    ]

    @pl.when(own)
    def _():
        for copy in local:
            copy.start()

    anc_local = pltpu.make_async_copy(anc_h, anc_s.at[k], an_l.at[0])
    anc_local.start()

    def rows_of(core, first, count):
        return pl.ds(pl.multiple_of(core * BLOCK + first, HALF), count)

    @pl.loop(0, BLOCK // 16)
    def _(i):
        rows = pl.ds(pl.multiple_of(i * 16, 16), 16)
        v = hid[rows, :].astype(F32)
        scale = lax.rsqrt(jnp.mean(v * v, axis=1, keepdims=True) + 1e-06)
        xb[0, pl.ds(pl.multiple_of(k * BLOCK + i * 16, 16), 16), :] = (v * scale * gain[...]).astype(BF16)

    pl.semaphore_wait(barrier, len(greeted))

    A, B = (0, HALF), (HALF, HALF)
    routes = [
        (0, 1, A, right), (0, 1, B, right), (0, 3, B, left), (0, 3, A, left), (0, 0, (0, BLOCK), sib),
        (1, 2, A, right), (3, 2, B, left),
        (1, 1, A, sib), (1, 1, B, sib), (3, 3, B, sib), (3, 3, A, sib), (2, 2, A, sib), (2, 2, B, sib),
    ]

    def ag(m):
        s, t, (first, count), to = routes[m]
        rows = rows_of(k, first, count)
        return send(xb.at[s, rows, :], xb.at[t, rows, :], ag_s.at[m], ag_r.at[m], to)

    for m in range(5):
        ag(m).start()

    anc_send = send(anc_h, anc_v, an_s.at[0], an_r.at[0], sib)
    anc_send.start()

    def chunk(n, quarter):
        def rows(size, part, parts):
            return pl.ds(pl.multiple_of(quarter * size + part * (size // parts), 16), size // parts)

        if n == 0:
            r = rows(D // 4, 0, 1)
            return wk_h.at[r, :], wkv.at[r, pl.ds(0, HDIM)]
        if n == 1:
            r = rows(D // 4, 0, 1)
            return wv_h.at[r, :], wkv.at[r, pl.ds(HDIM, HDIM)]
        if n in (2, 3):
            r = rows(D // 4, n - 2, 2)
            return wq_h.at[r, :], wq.at[r, :]
        r = rows(QCOLS // 4, n - 4, 2)
        return wo_h.at[r, :], wo.at[r, :]

    y_target = dev(x, (y + 3 + 2 * k) % 4, z, par)

    def w_out_send(n):
        quarter = 2 * zp + k
        src, dst = chunk(n, quarter)
        return send(src, dst, ws_s.at[n], ws_r.at[n, quarter], y_target)

    def w_arrival(n, quarter):
        _, dst = chunk(n, quarter)
        return send(dst, dst, ws_s.at[n], ws_r.at[n, quarter], y_target)

    def w_pass(n, side):
        quarter = 2 * zp + side
        _, dst = chunk(n, quarter)
        to = dev(x, y, (z + 1 + 2 * side) % 4, k)
        return send(dst, dst, wz_s.at[n, side], ws_r.at[n, quarter], to)

    def pass_weights(chunks):
        @pl.when(jnp.logical_not(own))
        def _():
            for n in chunks:
                for side in range(2):
                    w_arrival(n, 2 * zp + side).wait_recv()
                    w_pass(n, side).start()

    def wait_weights(chunks, locals_):
        @pl.when(own)
        def _():
            for i in locals_:
                local[i].wait()

        @pl.when(jnp.logical_not(own))
        def _():
            for n in chunks:
                for side in range(2):
                    w_arrival(n, 2 * (1 - zp) + side).wait_recv()

    for n in range(4):
        w_out_send(n).start()

    pass_weights((0, 1))

    def rope(block):
        cos_b, sin_b = cb[pl.ds(block, 1), :], sb[pl.ds(block, 1), :]
        cosine = cos_b * ci[...] - sin_b * si[...]
        sine = sin_b * ci[...] + cos_b * si[...]
        lane = lax.broadcasted_iota(jnp.int32, (BLOCK, HDIM), 1)
        return cosine, jnp.where(lane < HDIM // 2, -sine, sine)

    def rotated(v, table):
        return v * table[0] + pltpu.roll(v, HDIM // 2, 1) * table[1]

    def x_of(r):
        return (x + 4 - r) % 4

    def block_of(r, core):
        return 16 * span + 8 * core + 2 * x_of(r) + par

    def project_kv(r):
        both = jnp.dot(xb[r], wkv[...], preferred_element_type=F32)
        for core in range(2):
            part = both[core * BLOCK : (core + 1) * BLOCK]
            slot = 48 + 8 * par + 2 * x_of(r) + core
            kv[slot, 0] = rotated(part[:, :HDIM], rope(block_of(r, core))).astype(BF16)
            kv[slot, 1] = part[:, HDIM:].astype(BF16)

    def project_q(r):
        for first, count in ((0, 2), (2, 2), (4, 1)):
            got = jnp.dot(xb[r], wq[:, first * HDIM : (first + count) * HDIM], preferred_element_type=F32)
            for core in range(2):
                table = rope(block_of(r, core))
                for e in range(count):
                    part = got[core * BLOCK : (core + 1) * BLOCK, e * HDIM : (e + 1) * HDIM]
                    qs[r, core, first + e] = (rotated(part, table) * Q_SCALE).astype(BF16)

    def kv_pair(region, r):
        return kv.at[pl.ds(16 * region + 8 * par + 2 * x_of(r), 2)]

    def kv_sem(region, parity, r):
        return kv_r.at[region * 8 + parity * 4 + r]

    partner = dev(x, yh * 2 + 1 - par, z, k)

    def other(t):
        return dev(x, (1 - yh) * 2 + t, z, k)

    def kv_up(r):
        return send(kv_pair(3, r), kv_pair(1, r), kv_s.at[r], kv_sem(1, par, r), dev(x, y, (z + 1) % 4, k))

    def kv_partner(r):
        return send(kv_pair(3, r), kv_pair(3, r), kv_s.at[4 + r], kv_sem(3, par, r), partner)

    def kv_next(r, t):
        return send(kv_pair(3, r), kv_pair(2, r), kv_s.at[8 + 2 * r + t], kv_sem(2, par, r), other(t))

    def kv_pass_partner(r):
        return send(kv_pair(1, r), kv_pair(1, r), kv_s.at[16 + r], kv_sem(1, par, r), partner)

    def kv_pass_next(r, t):
        return send(kv_pair(1, r), kv_pair(2, r), kv_s.at[20 + 2 * r + t], kv_sem(2, par, r), other(t))

    def kv_far(i, t):
        slot = 8 * par + 5 + 2 * i
        to = dev(x, (1 - yh) * 2 + t, (z + yh) % 4, k)
        return send(kv.at[pl.ds(16 + slot, 1)], kv.at[pl.ds(slot, 1)], kv_s.at[28 + 2 * i + t], kv_sem(0, par, i), to)

    far_sends = jnp.logical_and(z > 0, z + yh < 4)

    def start_kv(r):
        @pl.when(z < 3)
        def _():
            kv_up(r).start()

        kv_partner(r).start()

        @pl.when(yh == 0)
        def _():
            for t in range(2):
                kv_next(r, t).start()

    def pass_kv(r):
        @pl.when(z > 0)
        def _():
            kv_up(r).wait_recv()
            kv_pass_partner(r).start()

            @pl.when(yh == 1)
            def _():
                for t in range(2):
                    kv_pass_next(r, t).start()

    ag(0).wait_recv()
    ag(5).start()
    ag(7).start()
    ag(2).wait_recv()
    ag(6).start()
    ag(9).start()
    pass_weights((2, 3))
    wait_weights((0, 1), (0, 1))
    ag(4).wait_recv()
    project_kv(0)
    ag(1).wait_recv()
    ag(8).start()
    ag(3).wait_recv()
    ag(10).start()
    for m in (7, 8, 9, 10):
        ag(m).wait_recv()

    @pl.loop(0, 2)
    def _(i):
        project_kv(1 + 2 * i)

    for r in (0, 1, 3):
        start_kv(r)
    for n in (4, 5):
        w_out_send(n).start()
    wait_weights((2, 3), (2,))

    @pl.loop(0, 3)
    def _(i):
        project_q(i + i // 2)

    for r in (0, 1, 3):
        pass_kv(r)
    for m in (5, 6):
        ag(m).wait_recv()
        ag(m + 6).start()
    for m in (11, 12):
        ag(m).wait_recv()
    project_kv(2)
    start_kv(2)
    project_q(2)
    pass_kv(2)

    @pl.when(far_sends)
    def _():
        for i in range(2):
            for t in range(2):
                kv_far(i, t).start()

    pass_weights((4, 5))
    for m in range(13):
        ag(m).wait_send()

    anc_local.wait()
    anc_send.wait()
    anc_move = pltpu.make_async_copy(anc_v, anc_s.at[1 - k], an_l.at[1])
    anc_move.start()
    anc_move.wait()

    def kv_arrival(region, parity, r, blocks):
        ref = kv.at[pl.ds(16 * region + 8 * parity + 2 * r, blocks)]
        return send(ref, ref, kv_s.at[0], kv_sem(region, parity, r), partner)

    for r in range(4):
        kv_arrival(3, 1 - par, r, 2).wait_recv()

    @pl.when(span >= 1)
    def _():
        for parity in range(2):
            for r in range(4):
                kv_arrival(2, parity, r, 2).wait_recv()

    @pl.when(span >= 2)
    def _():
        for r in range(4):
            kv_arrival(1, 1 - par, r, 2).wait_recv()

    @pl.when(span >= 3)
    def _():
        for parity in range(2):
            for i in range(2):
                kv_arrival(0, parity, i, 1).wait_recv()

    def attend(r):
        xr = x_of(r)

        @pl.loop(0, 2)
        def _(core):
            row = 2 * xr + par
            mine = 48 + 8 * par + 2 * xr + core
            keys, values, biases = [kv[mine, 0]], [kv[mine, 1]], [None]
            for j in range(MAXA):
                a = anc_s[core, row, j]
                listed = a >= 0
                place = jnp.where(listed, jnp.clip(a - 16 * span + 48, 0, 63), 48 + 8 * core + row)
                within = place % 16
                slot = (place // 16) * 16 + (within % 2) * 8 + ((within // 2) % 4) * 2 + within // 8
                keys.append(kv[slot, 0])
                values.append(kv[slot, 1])
                biases.append(jnp.where(listed, 0.0, -1e30).astype(F32))
            causal = lax.broadcasted_iota(jnp.int32, (BLOCK, BLOCK), 0) >= lax.broadcasted_iota(
                jnp.int32, (BLOCK, BLOCK), 1
            )
            for e in range(PER_GROUP):
                q = qs[r, core, e]
                scores = []
                for key, bias in zip(keys, biases):
                    s = lax.dot_general(q, key, (((1,), (1,)), ((), ())), preferred_element_type=F32)
                    scores.append(jnp.where(causal, s, -1e30) if bias is None else s + bias)
                top = functools.reduce(jnp.maximum, scores).max(axis=1, keepdims=True)
                weights = [jnp.exp2(s - top) for s in scores]
                total = functools.reduce(jnp.add, weights).sum(axis=1, keepdims=True)
                mixture = sum(
                    jnp.dot(w.astype(BF16), v, preferred_element_type=F32) for w, v in zip(weights, values)
                )
                att[rows_of(core, 0, BLOCK), e * HDIM : (e + 1) * HDIM] = (mixture / total).astype(BF16)

    def project_out(r):
        @pl.loop(0, D // N_OUT)
        def _(n):
            cols = pl.ds(pl.multiple_of(n * N_OUT, N_OUT), N_OUT)
            xb[r, :, cols] = jnp.dot(att[...], wo[:, cols], preferred_element_type=F32).astype(BF16)

    def to_sibling(r):
        return send(xb.at[r, rows_of(1 - k, 0, BLOCK), :], rb.at[r], rs_s.at[r], rs_r.at[r], sib)

    def add_into(r, first, count, terms):
        @pl.loop(0, count // 16)
        def _(i):
            at = pl.multiple_of(first + i * 16, 16)
            rows = pl.ds(pl.multiple_of(k * BLOCK + first + i * 16, 16), 16)
            total = xb[r, rows, :].astype(F32)
            for term in terms:
                total = total + term(at).astype(F32)
            xb[r, rows, :] = total.astype(BF16)

    def half(r, first):
        return xb.at[r, rows_of(k, first, HALF), :]

    def far_send(side):
        return send(half(2, side * HALF), far.at[side], rs_s.at[4 + side], rs_r.at[4 + side], (right, left)[side])

    def fin_send(side, first):
        n = 6 + 2 * side + first // HALF
        dst = fin.at[side, pl.ds(first, HALF), :]
        return send(half((3, 1)[side], first), dst, rs_s.at[n], rs_r.at[n], (right, left)[side])

    def take_sibling(r):
        to_sibling(r).wait_recv()
        add_into(r, 0, BLOCK, [lambda at: rb[r, pl.ds(at, 16), :]])

    attend(2)
    wait_weights((4, 5), (3,))
    project_out(2)
    to_sibling(2).start()
    attend(3)
    take_sibling(2)
    for side in range(2):
        far_send(side).start()
    project_out(3)
    to_sibling(3).start()
    attend(1)
    project_out(1)
    to_sibling(1).start()
    take_sibling(3)
    fin_send(0, HALF).start()
    take_sibling(1)
    fin_send(1, 0).start()
    attend(0)
    project_out(0)
    to_sibling(0).start()
    for side, r, first in ((0, 3, 0), (1, 1, HALF)):
        far_send(side).wait_recv()
        add_into(r, first, HALF, [lambda at: far[side, pl.ds(at - first, 16), :]])
        fin_send(side, first).start()
    to_sibling(0).wait_recv()
    for n, (side, first) in enumerate(((0, HALF), (1, 0), (0, 0), (1, HALF))):
        fin_send(side, first).wait_recv()

    @pl.loop(0, BLOCK // 16)
    def _(i):
        at = pl.ds(pl.multiple_of(i * 16, 16), 16)
        rows = pl.ds(pl.multiple_of(k * BLOCK + i * 16, 16), 16)
        total = xb[0, rows, :].astype(F32) + rb[0, at, :].astype(F32)
        total = total + fin[0, at, :].astype(F32) + fin[1, at, :].astype(F32)
        out[at, :] = total.astype(BF16)

    for r in range(4):
        to_sibling(r).wait_send()
        kv_partner(r).wait_send()
    for side in range(2):
        far_send(side).wait_send()
        for first in (0, HALF):
            fin_send(side, first).wait_send()
    for n in range(6):
        w_out_send(n).wait_send()

    @pl.when(jnp.logical_not(own))
    def _():
        for n in range(6):
            for side in range(2):
                w_pass(n, side).wait_send()

    @pl.when(z < 3)
    def _():
        for r in range(4):
            kv_up(r).wait_send()

    @pl.when(yh == 0)
    def _():
        for r in range(4):
            for t in range(2):
                kv_next(r, t).wait_send()

    @pl.when(z > 0)
    def _():
        for r in range(4):
            kv_pass_partner(r).wait_send()

    @pl.when(jnp.logical_and(z > 0, yh == 1))
    def _():
        for r in range(4):
            for t in range(2):
                kv_pass_next(r, t).wait_send()

    @pl.when(far_sends)
    def _():
        for i in range(2):
            for t in range(2):
                kv_far(i, t).wait_send()


def on_device(hidden_rows, norm_gain, w_query, w_key, w_value, w_out, ancestors):
    vmem = pl.BlockSpec(memory_space=pltpu.VMEM)
    hbm = pl.BlockSpec(memory_space=pl.ANY)
    dma = pltpu.SemaphoreType.DMA
    lists = jnp.pad(ancestors, ((0, 0), (0, 128 - MAXA)))
    return pl.pallas_call(
        kernel,
        out_shape=jax.ShapeDtypeStruct((BLOCK, D), BF16),
        in_specs=[vmem, vmem, hbm, hbm, hbm, hbm, hbm, vmem, vmem, vmem, vmem],
        out_specs=vmem,
        scratch_shapes=[
            pltpu.VMEM((4, 2 * BLOCK, D), BF16),
            pltpu.VMEM((D, 2 * HDIM), BF16),
            pltpu.VMEM((D, QCOLS), BF16),
            pltpu.VMEM((QCOLS, D), BF16),
            pltpu.VMEM((4, 2, PER_GROUP, BLOCK, HDIM), BF16),
            pltpu.VMEM((64, 2, BLOCK, HDIM), BF16),
            pltpu.VMEM((2 * BLOCK, QCOLS), BF16),
            pltpu.VMEM((4, BLOCK, D), BF16),
            pltpu.VMEM((2, HALF, D), BF16),
            pltpu.VMEM((2, BLOCK, D), BF16),
            pltpu.VMEM((8, 128), jnp.int32),
            pltpu.SMEM((2, 8, 128), jnp.int32),
            dma((13,)),
            dma((13,)),
            dma((6,)),
            dma((6, 4)),
            dma((6, 2)),
            dma((4,)),
            dma((32,)),
            dma((32,)),
            dma((10,)),
            dma((10,)),
            dma((1,)),
            dma((1,)),
            dma((2,)),
        ],
        compiler_params=pltpu.CompilerParams(
            collective_id=0, has_side_effects=True, vmem_limit_bytes=60 * 2**20
        ),
        cost_estimate=pl.CostEstimate(
            flops=17 * 10**9, bytes_accessed=20 * 10**6, transcendentals=4 * 10**6
        ),
    )(
        hidden_rows, norm_gain.reshape(1, D), w_query, w_key, w_value, w_out, lists,
        *[jnp.asarray(t) for t in rope_tables()],
    )


def solution(mesh):
    placed = (
        P(("ctx", "head"), None),
        P(),
        P(None, "head"),
        P(None, "head"),
        P(None, "head"),
        P("head", None),
        P("ctx", None),
    )
    return jax.shard_map(
        on_device, mesh=mesh, in_specs=placed, out_specs=P(("ctx", "head"), None), check_vma=False
    )
```

time: 919 us -> 160 us (0.17); the launches traced: 906 us -> 158 us
  waiting for transfers between devices: 578 us -> 0 us
  Pallas kernels: 0 us -> 154 us
  other arithmetic: 139 us -> 0 us
  local copies, waits for them, and re-layouts: 80.3 us -> 3.81 us
  matrix products: 63.4 us -> 0 us
  starting transfers between devices: 28.7 us -> 0 us
  between operations: 13.9 us -> 0.01 us
    reduce_scatter x1 -> x0, waiting for transfers between devices: 209 us -> none  [on_device(): lax.psum_scatter(jnp.dot(attended, w_out, preferred_element_type=jnp.floa...]
    all_gather x1 -> x0, waiting for transfers between devices: 203 us -> none  [on_device(): row_piece = lax.all_gather(normed, 'head', axis=0, tiled=True)]
    ppermute x15 -> x0, waiting for transfers between devices: 167 us -> none  [passed_along(): return lax.ppermute(block, axis, route)]
    pallas_call x0 -> x1, Pallas kernels: none -> 154 us  [on_device(): pl.pallas_call(kernel, out_shape=jax.ShapeDtypeStruct((BLOCK, D), BF16),...]
    select_n x49 -> x0, other arithmetic: 114 us -> none  [the longest x16 80.3 us: collect(): jnp.where(matches, value_pick, buffer_pair[1])]
    dot_general x6 -> x0, matrix products: 63.4 us -> none  [the longest x1 16.1 us: attend(): jnp.einsum('blgpe,bkge->bgplk', queries, all_keys, precision=lax.Precisio...]
    gather x32 -> x0, local copies, waits for them, and re-layouts: 43.4 us -> none  [the longest x16 32.5 us: collect(): jnp.take(passing[1].reshape(blocks, BLOCK, kv_cols), block_slot, axis=0)]
    ppermute x15 -> x0, starting transfers between devices: 28.6 us -> none  [passed_along(): return lax.ppermute(block, axis, route)]
  transfers between devices with their start and end apart: 17 -> 0, of which waited for: 17 -> 0; matrix products, arithmetic and copies ran while one was open for 1% -> 0% of each run, Pallas kernels for 0% -> 0%
where the time goes in v1:
time: 160 us; the launch traced here: 158 us
  Pallas kernels  154 us (96%)
  local copies, waits for them, and re-layouts  3.81 us (2%)
    pallas_call x1, Pallas kernels, on_device(): pl.pallas_call(kernel, out_shape=jax.ShapeDtypeStruct((BLOCK, D), BF16),...  154 us
    unnamed x2, local copies, waits for them, and re-layouts  3.21 us

profile of v1, /device:TPU:104, one launch (start us, length us, event | category | flops | bytes accessed | tf_op | source)
XLA Modules:
  0.0 158.2 jit_solution(136146897336528001)
XLA Ops:
  0.0 0.8 copy.12
  0.8 0.6 pad.4.anc_h
  1.4 154.3 %shard_map.109 = bf16[128,5120]{1,0:T(8,128)(2,1)} custom-call(bf16[128,5120]{1,0:T(8,128)(2,1)} %hid.1, f32[1,5120]{1,0:T(1,128)} %bitcast.1, bf16[5120,640]{1,0:T(8,128)(2,1)} %wq_h.1, bf16[5120,128]{1,0:T(8,128)(2,1)} %wk_h.1, bf16[5120,128]{1,0:T(8,128)(2,1)} %wv_h.1, bf16[640,5120]{1,0:T(8,128)(2,1)} %wo_h.1, s32[8,128]{1,0:T(8,128)} %pad.4.anc_h, ...), custom_call_target="tpu_custom_call" | custom-call | flops 16999999488 | bytes 20000000 | tf_op jit(solution)/shard_map/pallas_call | solution.py:501
  155.7 2.5 %copy.14 = bf16[128,5120]{1,0:T(8,128)(2,1)} copy(bf16[128,5120]{1,0:T(8,128)(2,1)} %shard_map.109) | data formatting | bytes 2621440

commit v2 on v1

--- a/solution.py
+++ b/solution.py
@@ -21,6 +21,7 @@
 F32 = jnp.float32
 BF16 = jnp.bfloat16
 N_OUT = 512
+WIDE = D // 2
 
 
 def rope_tables():
@@ -62,10 +63,13 @@
         )
 
     barrier = pltpu.get_barrier_semaphore()
-    greeted = [right, left, sib]
-    greeted += [dev(x, (y + d) % 4, z, k) for d in (1, 2, 3)]
+    partner = dev(x, yh * 2 + 1 - par, z, k)
+    cross_y = (1 - yh) * 2 + 1 - par
+    cross = dev(x, cross_y, z, k)
+    above = dev(x, y, (z + 1) % 4, k)
+    greeted = [right, left, sib, partner, cross, above, dev(x, y, (z + 3) % 4, k)]
     greeted += [dev(x, (y + d) % 4, z, 1 - k) for d in (1, 3)]
-    greeted += [dev(x, (y + d) % 4, (z + e) % 4, k) for e in (1, 3) for d in range(4)]
+    greeted += [dev(x, cross_y, (z + 3 + 2 * yh) % 4, k)]
     for to in greeted:
         pl.semaphore_signal(barrier, 1, device_id=to, device_id_type=MESH)
 
@@ -127,8 +131,9 @@
         if n in (2, 3):
             r = rows(D // 4, n - 2, 2)
             return wq_h.at[r, :], wq.at[r, :]
-        r = rows(QCOLS // 4, n - 4, 2)
-        return wo_h.at[r, :], wo.at[r, :]
+        r = rows(QCOLS // 4, 0, 1)
+        cols = pl.ds((n - 4) * WIDE, WIDE)
+        return wo_h.at[r, cols], wo.at[r, cols]
 
     y_target = dev(x, (y + 3 + 2 * k) % 4, z, par)
 
@@ -167,7 +172,7 @@
                 for side in range(2):
                     w_arrival(n, 2 * (1 - zp) + side).wait_recv()
 
-    for n in range(4):
+    for n in range(5):
         w_out_send(n).start()
 
     pass_weights((0, 1))
@@ -205,36 +210,35 @@
                     part = got[core * BLOCK : (core + 1) * BLOCK, e * HDIM : (e + 1) * HDIM]
                     qs[r, core, first + e] = (rotated(part, table) * Q_SCALE).astype(BF16)
 
-    def kv_pair(region, r):
-        return kv.at[pl.ds(16 * region + 8 * par + 2 * x_of(r), 2)]
-
-    def kv_sem(region, parity, r):
-        return kv_r.at[region * 8 + parity * 4 + r]
-
-    partner = dev(x, yh * 2 + 1 - par, z, k)
-
-    def other(t):
-        return dev(x, (1 - yh) * 2 + t, z, k)
+    def kv_pair(region, parity, r):
+        return kv.at[pl.ds(16 * region + 8 * parity + 2 * x_of(r), 2)]
+
+    def kv_send(n, src, dst, parity, r, to):
+        return send(
+            kv_pair(src, parity, r), kv_pair(dst, parity, r), kv_s.at[n], kv_r.at[dst * 8 + parity * 4 + r], to
+        )
 
     def kv_up(r):
-        return send(kv_pair(3, r), kv_pair(1, r), kv_s.at[r], kv_sem(1, par, r), dev(x, y, (z + 1) % 4, k))
-
-    def kv_partner(r):
-        return send(kv_pair(3, r), kv_pair(3, r), kv_s.at[4 + r], kv_sem(3, par, r), partner)
-
-    def kv_next(r, t):
-        return send(kv_pair(3, r), kv_pair(2, r), kv_s.at[8 + 2 * r + t], kv_sem(2, par, r), other(t))
-
-    def kv_pass_partner(r):
-        return send(kv_pair(1, r), kv_pair(1, r), kv_s.at[16 + r], kv_sem(1, par, r), partner)
-
-    def kv_pass_next(r, t):
-        return send(kv_pair(1, r), kv_pair(2, r), kv_s.at[20 + 2 * r + t], kv_sem(2, par, r), other(t))
-
-    def kv_far(i, t):
-        slot = 8 * par + 5 + 2 * i
-        to = dev(x, (1 - yh) * 2 + t, (z + yh) % 4, k)
-        return send(kv.at[pl.ds(16 + slot, 1)], kv.at[pl.ds(slot, 1)], kv_s.at[28 + 2 * i + t], kv_sem(0, par, i), to)
+        return kv_send(r, 3, 1, par, r, above)
+
+    def kv_partner(r, region):
+        return kv_send((16 if region == 1 else 4) + r, region, region, par, r, partner)
+
+    def kv_cross(r, region, mine):
+        parity = par if mine else 1 - par
+        return kv_send((20 if region == 1 else 8) + 2 * r + mine, region, 2, parity, r, cross)
+
+    def kv_from_partner(r, region):
+        return kv_send(0, region, region, 1 - par, r, partner)
+
+    def kv_far(i, mine):
+        parity = par if mine else 1 - par
+        slot = 8 * parity + 5 + 2 * i
+        to = dev(x, cross_y, (z + yh) % 4, k)
+        return send(
+            kv.at[pl.ds(16 + slot, 1)], kv.at[pl.ds(slot, 1)],
+            kv_s.at[28 + 2 * i + mine], kv_r.at[parity * 4 + i], to,
+        )
 
     far_sends = jnp.logical_and(z > 0, z + yh < 4)
 
@@ -243,23 +247,36 @@
         def _():
             kv_up(r).start()
 
-        kv_partner(r).start()
+        kv_partner(r, 3).start()
 
         @pl.when(yh == 0)
         def _():
-            for t in range(2):
-                kv_next(r, t).start()
+            kv_cross(r, 3, 1).start()
 
     def pass_kv(r):
         @pl.when(z > 0)
         def _():
             kv_up(r).wait_recv()
-            kv_pass_partner(r).start()
+            kv_partner(r, 1).start()
 
             @pl.when(yh == 1)
             def _():
-                for t in range(2):
-                    kv_pass_next(r, t).start()
+                kv_cross(r, 1, 1).start()
+
+    def pass_partner_kv(r):
+        kv_from_partner(r, 3).wait_recv()
+
+        @pl.when(yh == 0)
+        def _():
+            kv_cross(r, 3, 0).start()
+
+        @pl.when(z > 0)
+        def _():
+            kv_from_partner(r, 1).wait_recv()
+
+            @pl.when(yh == 1)
+            def _():
+                kv_cross(r, 1, 0).start()
 
     ag(0).wait_recv()
     ag(5).start()
@@ -284,8 +301,8 @@
 
     for r in (0, 1, 3):
         start_kv(r)
-    for n in (4, 5):
-        w_out_send(n).start()
+    w_out_send(5).start()
+    pass_weights((4,))
     wait_weights((2, 3), (2,))
 
     @pl.loop(0, 3)
@@ -294,6 +311,8 @@
 
     for r in (0, 1, 3):
         pass_kv(r)
+    for r in (0, 1, 3):
+        pass_partner_kv(r)
     for m in (5, 6):
         ag(m).wait_recv()
         ag(m + 6).start()
@@ -303,14 +322,14 @@
     start_kv(2)
     project_q(2)
     pass_kv(2)
+    pass_partner_kv(2)
 
     @pl.when(far_sends)
     def _():
         for i in range(2):
-            for t in range(2):
-                kv_far(i, t).start()
-
-    pass_weights((4, 5))
+            for mine in range(2):
+                kv_far(i, mine).start()
+
     for m in range(13):
         ag(m).wait_send()
 
@@ -322,21 +341,13 @@
 
     def kv_arrival(region, parity, r, blocks):
         ref = kv.at[pl.ds(16 * region + 8 * parity + 2 * r, blocks)]
-        return send(ref, ref, kv_s.at[0], kv_sem(region, parity, r), partner)
-
-    for r in range(4):
-        kv_arrival(3, 1 - par, r, 2).wait_recv()
+        return send(ref, ref, kv_s.at[0], kv_r.at[region * 8 + parity * 4 + r], partner)
 
     @pl.when(span >= 1)
     def _():
         for parity in range(2):
             for r in range(4):
                 kv_arrival(2, parity, r, 2).wait_recv()
-
-    @pl.when(span >= 2)
-    def _():
-        for r in range(4):
-            kv_arrival(1, 1 - par, r, 2).wait_recv()
 
     @pl.when(span >= 3)
     def _():
@@ -376,85 +387,105 @@
                 mixture = sum(
                     jnp.dot(w.astype(BF16), v, preferred_element_type=F32) for w, v in zip(weights, values)
                 )
-                att[rows_of(core, 0, BLOCK), e * HDIM : (e + 1) * HDIM] = (mixture / total).astype(BF16)
-
-    def project_out(r):
-        @pl.loop(0, D // N_OUT)
+                att[r, rows_of(core, 0, BLOCK), e * HDIM : (e + 1) * HDIM] = (mixture / total).astype(BF16)
+
+    def wide(j):
+        return pl.ds(j * WIDE, WIDE)
+
+    def project_out(r, j):
+        @pl.loop(0, WIDE // N_OUT)
         def _(n):
-            cols = pl.ds(pl.multiple_of(n * N_OUT, N_OUT), N_OUT)
-            xb[r, :, cols] = jnp.dot(att[...], wo[:, cols], preferred_element_type=F32).astype(BF16)
-
-    def to_sibling(r):
-        return send(xb.at[r, rows_of(1 - k, 0, BLOCK), :], rb.at[r], rs_s.at[r], rs_r.at[r], sib)
-
-    def add_into(r, first, count, terms):
+            cols = pl.ds(pl.multiple_of(j * WIDE + n * N_OUT, N_OUT), N_OUT)
+            xb[r, :, cols] = jnp.dot(att[r], wo[:, cols], preferred_element_type=F32).astype(BF16)
+
+    def to_sibling(r, j):
+        n = 4 * j + r
+        src = xb.at[r, rows_of(1 - k, 0, BLOCK), wide(j)]
+        return send(src, rb.at[r, :, wide(j)], rs_s.at[n], rs_r.at[n], sib)
+
+    def add_into(r, j, first, count, term):
         @pl.loop(0, count // 16)
         def _(i):
-            at = pl.multiple_of(first + i * 16, 16)
+            at = pl.ds(pl.multiple_of(i * 16, 16), 16)
             rows = pl.ds(pl.multiple_of(k * BLOCK + first + i * 16, 16), 16)
-            total = xb[r, rows, :].astype(F32)
-            for term in terms:
-                total = total + term(at).astype(F32)
-            xb[r, rows, :] = total.astype(BF16)
-
-    def half(r, first):
-        return xb.at[r, rows_of(k, first, HALF), :]
-
-    def far_send(side):
-        return send(half(2, side * HALF), far.at[side], rs_s.at[4 + side], rs_r.at[4 + side], (right, left)[side])
-
-    def fin_send(side, first):
-        n = 6 + 2 * side + first // HALF
-        dst = fin.at[side, pl.ds(first, HALF), :]
-        return send(half((3, 1)[side], first), dst, rs_s.at[n], rs_r.at[n], (right, left)[side])
-
-    def take_sibling(r):
-        to_sibling(r).wait_recv()
-        add_into(r, 0, BLOCK, [lambda at: rb[r, pl.ds(at, 16), :]])
+            total = xb[r, rows, wide(j)].astype(F32) + term[at, wide(j)].astype(F32)
+            xb[r, rows, wide(j)] = total.astype(BF16)
+
+    def half(r, j, first):
+        return xb.at[r, rows_of(k, first, HALF), wide(j)]
+
+    def far_send(side, j):
+        n = 8 + 2 * j + side
+        return send(half(2, j, side * HALF), far.at[side, :, wide(j)], rs_s.at[n], rs_r.at[n], (right, left)[side])
+
+    def fin_send(side, j, first):
+        n = 12 + 4 * j + 2 * side + first // HALF
+        dst = fin.at[side, pl.ds(first, HALF), wide(j)]
+        return send(half((3, 1)[side], j, first), dst, rs_s.at[n], rs_r.at[n], (right, left)[side])
+
+    def take_sibling(r, j):
+        to_sibling(r, j).wait_recv()
+        add_into(r, j, 0, BLOCK, rb.at[r])
+
+    def put_out(r, j):
+        project_out(r, j)
+        to_sibling(r, j).start()
+
+    def open_half(j, attend):
+        put_out(2, j)
+        attend(3)
+        take_sibling(2, j)
+        for side in range(2):
+            far_send(side, j).start()
+        put_out(3, j)
+        attend(1)
+        put_out(1, j)
+        take_sibling(3, j)
+        fin_send(0, j, HALF).start()
+        take_sibling(1, j)
+        fin_send(1, j, 0).start()
+        attend(0)
+        put_out(0, j)
+
+    def close_half(j):
+        for side, r, first in ((0, 3, 0), (1, 1, HALF)):
+            far_send(side, j).wait_recv()
+            add_into(r, j, first, HALF, far.at[side])
+            fin_send(side, j, first).start()
+
+    def finish(j):
+        to_sibling(0, j).wait_recv()
+        for side, first in ((0, HALF), (1, 0), (0, 0), (1, HALF)):
+            fin_send(side, j, first).wait_recv()
+
+        @pl.loop(0, BLOCK // 16)
+        def _(i):
+            at = pl.ds(pl.multiple_of(i * 16, 16), 16)
+            rows = pl.ds(pl.multiple_of(k * BLOCK + i * 16, 16), 16)
+            total = xb[0, rows, wide(j)].astype(F32) + rb[0, at, wide(j)].astype(F32)
+            total = total + fin[0, at, wide(j)].astype(F32) + fin[1, at, wide(j)].astype(F32)
+            out[at, wide(j)] = total.astype(BF16)
 
     attend(2)
-    wait_weights((4, 5), (3,))
-    project_out(2)
-    to_sibling(2).start()
-    attend(3)
-    take_sibling(2)
-    for side in range(2):
-        far_send(side).start()
-    project_out(3)
-    to_sibling(3).start()
-    attend(1)
-    project_out(1)
-    to_sibling(1).start()
-    take_sibling(3)
-    fin_send(0, HALF).start()
-    take_sibling(1)
-    fin_send(1, 0).start()
-    attend(0)
-    project_out(0)
-    to_sibling(0).start()
-    for side, r, first in ((0, 3, 0), (1, 1, HALF)):
-        far_send(side).wait_recv()
-        add_into(r, first, HALF, [lambda at: far[side, pl.ds(at - first, 16), :]])
-        fin_send(side, first).start()
-    to_sibling(0).wait_recv()
-    for n, (side, first) in enumerate(((0, HALF), (1, 0), (0, 0), (1, HALF))):
-        fin_send(side, first).wait_recv()
-
-    @pl.loop(0, BLOCK // 16)
-    def _(i):
-        at = pl.ds(pl.multiple_of(i * 16, 16), 16)
-        rows = pl.ds(pl.multiple_of(k * BLOCK + i * 16, 16), 16)
-        total = xb[0, rows, :].astype(F32) + rb[0, at, :].astype(F32)
-        total = total + fin[0, at, :].astype(F32) + fin[1, at, :].astype(F32)
-        out[at, :] = total.astype(BF16)
+    wait_weights((4,), (3,))
+    open_half(0, attend)
+    pass_weights((5,))
+    close_half(0)
+    wait_weights((5,), ())
+    open_half(1, lambda r: None)
+    finish(0)
+    close_half(1)
+    finish(1)
 
     for r in range(4):
-        to_sibling(r).wait_send()
-        kv_partner(r).wait_send()
-    for side in range(2):
-        far_send(side).wait_send()
-        for first in (0, HALF):
-            fin_send(side, first).wait_send()
+        for j in range(2):
+            to_sibling(r, j).wait_send()
+        kv_partner(r, 3).wait_send()
+    for j in range(2):
+        for side in range(2):
+            far_send(side, j).wait_send()
+            for first in (0, HALF):
+                fin_send(side, j, first).wait_send()
     for n in range(6):
         w_out_send(n).wait_send()
 
@@ -472,25 +503,25 @@
     @pl.when(yh == 0)
     def _():
         for r in range(4):
-            for t in range(2):
-                kv_next(r, t).wait_send()
+            for mine in range(2):
+                kv_cross(r, 3, mine).wait_send()
 
     @pl.when(z > 0)
     def _():
         for r in range(4):
-            kv_pass_partner(r).wait_send()
+            kv_partner(r, 1).wait_send()
 
     @pl.when(jnp.logical_and(z > 0, yh == 1))
     def _():
         for r in range(4):
-            for t in range(2):
-                kv_pass_next(r, t).wait_send()
+            for mine in range(2):
+                kv_cross(r, 1, mine).wait_send()
 
     @pl.when(far_sends)
     def _():
         for i in range(2):
-            for t in range(2):
-                kv_far(i, t).wait_send()
+            for mine in range(2):
+                kv_far(i, mine).wait_send()
 
 
 def on_device(hidden_rows, norm_gain, w_query, w_key, w_value, w_out, ancestors):
@@ -510,7 +541,7 @@
             pltpu.VMEM((QCOLS, D), BF16),
             pltpu.VMEM((4, 2, PER_GROUP, BLOCK, HDIM), BF16),
             pltpu.VMEM((64, 2, BLOCK, HDIM), BF16),
-            pltpu.VMEM((2 * BLOCK, QCOLS), BF16),
+            pltpu.VMEM((4, 2 * BLOCK, QCOLS), BF16),
             pltpu.VMEM((4, BLOCK, D), BF16),
             pltpu.VMEM((2, HALF, D), BF16),
             pltpu.VMEM((2, BLOCK, D), BF16),
@@ -524,8 +555,8 @@
             dma((4,)),
             dma((32,)),
             dma((32,)),
-            dma((10,)),
-            dma((10,)),
+            dma((20,)),
+            dma((20,)),
             dma((1,)),
             dma((1,)),
             dma((2,)),

time: 160 us -> 160 us (level)
  the two profiles are of different devices: /device:TPU:104 before, /device:TPU:0 now
where the time goes in v2:
time: 160 us
  Pallas kernels  156 us (98%)
  local copies, waits for them, and re-layouts  3.81 us (2%)
    pallas_call x1, Pallas kernels, on_device(): pl.pallas_call(kernel, out_shape=jax.ShapeDtypeStruct((BLOCK, D), BF16),...  156 us
    unnamed x2, local copies, waits for them, and re-layouts  3.21 us

profile of v2, /device:TPU:0, one launch (start us, length us, event | category | flops | bytes accessed | tf_op | source)
XLA Modules:
  0.0 160.2 jit_solution(7817540929307271397)
XLA Ops:
  0.0 0.8 copy.12
  0.8 0.6 pad.4.anc_h
  1.4 156.4 %shard_map.109 = bf16[128,5120]{1,0:T(8,128)(2,1)} custom-call(bf16[128,5120]{1,0:T(8,128)(2,1)} %hid.1, f32[1,5120]{1,0:T(1,128)} %bitcast.1, bf16[5120,640]{1,0:T(8,128)(2,1)} %wq_h.1, bf16[5120,128]{1,0:T(8,128)(2,1)} %wk_h.1, bf16[5120,128]{1,0:T(8,128)(2,1)} %wv_h.1, bf16[640,5120]{1,0:T(8,128)(2,1)} %wo_h.1, s32[8,128]{1,0:T(8,128)} %pad.4.anc_h, ...), custom_call_target="tpu_custom_call" | custom-call | flops 16999999488 | bytes 20000000 | tf_op jit(solution)/shard_map/pallas_call | solution.py:532
  157.7 2.5 %copy.14 = bf16[128,5120]{1,0:T(8,128)(2,1)} copy(bf16[128,5120]{1,0:T(8,128)(2,1)} %shard_map.109) | data formatting | bytes 2621440

commit v3 on v2

--- a/solution.py
+++ b/solution.py
@@ -69,7 +69,10 @@
     above = dev(x, y, (z + 1) % 4, k)
     greeted = [right, left, sib, partner, cross, above, dev(x, y, (z + 3) % 4, k)]
     greeted += [dev(x, (y + d) % 4, z, 1 - k) for d in (1, 3)]
-    greeted += [dev(x, cross_y, (z + 3 + 2 * yh) % 4, k)]
+    opposite_y = (1 - yh) * 2 + par
+    opposite = dev(x, opposite_y, z, k)
+    next_z = (z + 3 + 2 * yh) % 4
+    greeted += [opposite, dev(x, cross_y, next_z, k), dev(x, opposite_y, next_z, k)]
     for to in greeted:
         pl.semaphore_signal(barrier, 1, device_id=to, device_id_type=MESH)
 
@@ -172,7 +175,7 @@
                 for side in range(2):
                     w_arrival(n, 2 * (1 - zp) + side).wait_recv()
 
-    for n in range(5):
+    for n in range(6):
         w_out_send(n).start()
 
     pass_weights((0, 1))
@@ -224,6 +227,9 @@
     def kv_partner(r, region):
         return kv_send((16 if region == 1 else 4) + r, region, region, par, r, partner)
 
+    def kv_opposite(region):
+        return kv_send(32 + region // 3, region, 2, par, 2, opposite)
+
     def kv_cross(r, region, mine):
         parity = par if mine else 1 - par
         return kv_send((20 if region == 1 else 8) + 2 * r + mine, region, 2, parity, r, cross)
@@ -231,13 +237,12 @@
     def kv_from_partner(r, region):
         return kv_send(0, region, region, 1 - par, r, partner)
 
-    def kv_far(i, mine):
-        parity = par if mine else 1 - par
-        slot = 8 * parity + 5 + 2 * i
-        to = dev(x, cross_y, (z + yh) % 4, k)
+    def kv_far(i, t):
+        slot = 8 * par + 5 + 2 * i
+        to = dev(x, (cross_y, opposite_y)[t], (z + yh) % 4, k)
         return send(
             kv.at[pl.ds(16 + slot, 1)], kv.at[pl.ds(slot, 1)],
-            kv_s.at[28 + 2 * i + mine], kv_r.at[parity * 4 + i], to,
+            kv_s.at[28 + 2 * i + t], kv_r.at[par * 4 + i], to,
         )
 
     far_sends = jnp.logical_and(z > 0, z + yh < 4)
@@ -252,6 +257,8 @@
         @pl.when(yh == 0)
         def _():
             kv_cross(r, 3, 1).start()
+            if r == 2:
+                kv_opposite(3).start()
 
     def pass_kv(r):
         @pl.when(z > 0)
@@ -262,6 +269,8 @@
             @pl.when(yh == 1)
             def _():
                 kv_cross(r, 1, 1).start()
+                if r == 2:
+                    kv_opposite(1).start()
 
     def pass_partner_kv(r):
         kv_from_partner(r, 3).wait_recv()
@@ -301,7 +310,6 @@
 
     for r in (0, 1, 3):
         start_kv(r)
-    w_out_send(5).start()
     pass_weights((4,))
     wait_weights((2, 3), (2,))
 
@@ -322,14 +330,14 @@
     start_kv(2)
     project_q(2)
     pass_kv(2)
-    pass_partner_kv(2)
 
     @pl.when(far_sends)
     def _():
         for i in range(2):
-            for mine in range(2):
-                kv_far(i, mine).start()
-
+            for t in range(2):
+                kv_far(i, t).start()
+
+    pass_weights((5,))
     for m in range(13):
         ag(m).wait_send()
 
@@ -342,6 +350,12 @@
     def kv_arrival(region, parity, r, blocks):
         ref = kv.at[pl.ds(16 * region + 8 * parity + 2 * r, blocks)]
         return send(ref, ref, kv_s.at[0], kv_r.at[region * 8 + parity * 4 + r], partner)
+
+    kv_from_partner(2, 3).wait_recv()
+
+    @pl.when(z > 0)
+    def _():
+        kv_from_partner(2, 1).wait_recv()
 
     @pl.when(span >= 1)
     def _():
@@ -469,7 +483,6 @@
     attend(2)
     wait_weights((4,), (3,))
     open_half(0, attend)
-    pass_weights((5,))
     close_half(0)
     wait_weights((5,), ())
     open_half(1, lambda r: None)
@@ -502,8 +515,9 @@
 
     @pl.when(yh == 0)
     def _():
+        kv_opposite(3).wait_send()
         for r in range(4):
-            for mine in range(2):
+            for mine in range(r == 2, 2):
                 kv_cross(r, 3, mine).wait_send()
 
     @pl.when(z > 0)
@@ -513,15 +527,16 @@
 
     @pl.when(jnp.logical_and(z > 0, yh == 1))
     def _():
+        kv_opposite(1).wait_send()
         for r in range(4):
-            for mine in range(2):
+            for mine in range(r == 2, 2):
                 kv_cross(r, 1, mine).wait_send()
 
     @pl.when(far_sends)
     def _():
         for i in range(2):
-            for mine in range(2):
-                kv_far(i, mine).wait_send()
+            for t in range(2):
+                kv_far(i, t).wait_send()
 
 
 def on_device(hidden_rows, norm_gain, w_query, w_key, w_value, w_out, ancestors):
@@ -553,7 +568,7 @@
             dma((6, 4)),
             dma((6, 2)),
             dma((4,)),
-            dma((32,)),
+            dma((34,)),
             dma((32,)),
             dma((20,)),
             dma((20,)),

time: 160 us -> 150 us (0.938)
  the two profiles are of different devices: /device:TPU:0 before, /device:TPU:104 now
where the time goes in v3:
time: 150 us
  Pallas kernels  146 us (97%)
  local copies, waits for them, and re-layouts  3.81 us (3%)
    pallas_call x1, Pallas kernels, on_device(): pl.pallas_call(kernel, out_shape=jax.ShapeDtypeStruct((BLOCK, D), BF16),...  146 us
    unnamed x2, local copies, waits for them, and re-layouts  3.21 us

profile of v3, /device:TPU:104, one launch (start us, length us, event | category | flops | bytes accessed | tf_op | source)
XLA Modules:
  0.0 149.6 jit_solution(14832622319783331952)
XLA Ops:
  0.0 0.8 copy.12
  0.8 0.6 pad.4.anc_h
  1.4 145.8 %shard_map.109 = bf16[128,5120]{1,0:T(8,128)(2,1)} custom-call(bf16[128,5120]{1,0:T(8,128)(2,1)} %hid.1, f32[1,5120]{1,0:T(1,128)} %bitcast.1, bf16[5120,640]{1,0:T(8,128)(2,1)} %wq_h.1, bf16[5120,128]{1,0:T(8,128)(2,1)} %wk_h.1, bf16[5120,128]{1,0:T(8,128)(2,1)} %wv_h.1, bf16[640,5120]{1,0:T(8,128)(2,1)} %wo_h.1, s32[8,128]{1,0:T(8,128)} %pad.4.anc_h, ...), custom_call_target="tpu_custom_call" | custom-call | flops 16999999488 | bytes 20000000 | tf_op jit(solution)/shard_map/pallas_call | solution.py:547
  147.1 2.5 %copy.14 = bf16[128,5120]{1,0:T(8,128)(2,1)} copy(bf16[128,5120]{1,0:T(8,128)(2,1)} %shard_map.109) | data formatting | bytes 2621440

commit v4 on v3

--- a/solution.py
+++ b/solution.py
@@ -20,8 +20,9 @@
 MESH = pl.DeviceIdType.MESH
 F32 = jnp.float32
 BF16 = jnp.bfloat16
-N_OUT = 512
+N_OUT = 1280
 WIDE = D // 2
+ROWS = 64
 
 
 def rope_tables():
@@ -35,7 +36,7 @@
 def kernel(
     hid, gain, wq_h, wk_h, wv_h, wo_h, anc_h, ci, si, cb, sb,
     out,
-    xb, wkv, wq, wo, qs, kv, att, rb, far, fin, anc_v, anc_s,
+    xb, wkv, wq, wo, qs, kv, att, rb, far, fin, kc, vc, scores, probs, share, anc_v, anc_s,
     ag_s, ag_r, ws_s, ws_r, wz_s, wl, kv_s, kv_r, rs_s, rs_r, an_s, an_r, an_l,
 ):
     c = lax.axis_index("ctx")
@@ -313,14 +314,10 @@
     pass_weights((4,))
     wait_weights((2, 3), (2,))
 
-    @pl.loop(0, 3)
-    def _(i):
-        project_q(i + i // 2)
-
+    project_q(0)
     for r in (0, 1, 3):
         pass_kv(r)
-    for r in (0, 1, 3):
-        pass_partner_kv(r)
+    project_q(1)
     for m in (5, 6):
         ag(m).wait_recv()
         ag(m + 6).start()
@@ -328,7 +325,8 @@
         ag(m).wait_recv()
     project_kv(2)
     start_kv(2)
-    project_q(2)
+    for r in (0, 1, 3):
+        pass_partner_kv(r)
     pass_kv(2)
 
     @pl.when(far_sends)
@@ -338,6 +336,11 @@
                 kv_far(i, t).start()
 
     pass_weights((5,))
+
+    @pl.loop(2, 4)
+    def _(i):
+        project_q(i)
+
     for m in range(13):
         ag(m).wait_send()
 
@@ -376,32 +379,39 @@
         def _(core):
             row = 2 * xr + par
             mine = 48 + 8 * par + 2 * xr + core
-            keys, values, biases = [kv[mine, 0]], [kv[mine, 1]], [None]
+            kc[0:BLOCK, :] = kv[mine, 0]
+            vc[0:BLOCK, :] = kv[mine, 1]
+            biases = []
             for j in range(MAXA):
                 a = anc_s[core, row, j]
                 listed = a >= 0
                 place = jnp.where(listed, jnp.clip(a - 16 * span + 48, 0, 63), 48 + 8 * core + row)
                 within = place % 16
                 slot = (place // 16) * 16 + (within % 2) * 8 + ((within // 2) % 4) * 2 + within // 8
-                keys.append(kv[slot, 0])
-                values.append(kv[slot, 1])
+                kc[(j + 1) * BLOCK : (j + 2) * BLOCK, :] = kv[slot, 0]
+                vc[(j + 1) * BLOCK : (j + 2) * BLOCK, :] = kv[slot, 1]
                 biases.append(jnp.where(listed, 0.0, -1e30).astype(F32))
-            causal = lax.broadcasted_iota(jnp.int32, (BLOCK, BLOCK), 0) >= lax.broadcasted_iota(
-                jnp.int32, (BLOCK, BLOCK), 1
-            )
+            q = qs[r, core].reshape(QCOLS, HDIM)
+            scores[...] = lax.dot_general(q, kc[...], (((1,), (1,)), ((), ())), preferred_element_type=F32)
+            for first in range(0, QCOLS, ROWS):
+                rows = slice(first, first + ROWS)
+                causal = lax.broadcasted_iota(jnp.int32, (ROWS, BLOCK), 0) + first % BLOCK >= (
+                    lax.broadcasted_iota(jnp.int32, (ROWS, BLOCK), 1)
+                )
+                parts = [jnp.where(causal, scores[rows, 0:BLOCK], -1e30)]
+                for j in range(MAXA):
+                    parts.append(scores[rows, (j + 1) * BLOCK : (j + 2) * BLOCK] + biases[j])
+                top = functools.reduce(jnp.maximum, parts).max(axis=1, keepdims=True)
+                parts = [jnp.exp2(part - top) for part in parts]
+                total = functools.reduce(jnp.add, parts).sum(axis=1, keepdims=True)
+                share[rows, :] = jnp.broadcast_to(1.0 / total, (ROWS, HDIM))
+                for j in range(MAXA + 1):
+                    probs[rows, j * BLOCK : (j + 1) * BLOCK] = parts[j].astype(BF16)
+            mixture = jnp.dot(probs[...], vc[...], preferred_element_type=F32) * share[...]
             for e in range(PER_GROUP):
-                q = qs[r, core, e]
-                scores = []
-                for key, bias in zip(keys, biases):
-                    s = lax.dot_general(q, key, (((1,), (1,)), ((), ())), preferred_element_type=F32)
-                    scores.append(jnp.where(causal, s, -1e30) if bias is None else s + bias)
-                top = functools.reduce(jnp.maximum, scores).max(axis=1, keepdims=True)
-                weights = [jnp.exp2(s - top) for s in scores]
-                total = functools.reduce(jnp.add, weights).sum(axis=1, keepdims=True)
-                mixture = sum(
-                    jnp.dot(w.astype(BF16), v, preferred_element_type=F32) for w, v in zip(weights, values)
-                )
-                att[r, rows_of(core, 0, BLOCK), e * HDIM : (e + 1) * HDIM] = (mixture / total).astype(BF16)
+                att[r, rows_of(core, 0, BLOCK), e * HDIM : (e + 1) * HDIM] = mixture[
+                    e * BLOCK : (e + 1) * BLOCK
+                ].astype(BF16)
 
     def wide(j):
         return pl.ds(j * WIDE, WIDE)
@@ -560,6 +570,11 @@
             pltpu.VMEM((4, BLOCK, D), BF16),
             pltpu.VMEM((2, HALF, D), BF16),
             pltpu.VMEM((2, BLOCK, D), BF16),
+            pltpu.VMEM(((MAXA + 1) * BLOCK, HDIM), BF16),
+            pltpu.VMEM(((MAXA + 1) * BLOCK, HDIM), BF16),
+            pltpu.VMEM((QCOLS, (MAXA + 1) * BLOCK), F32),
+            pltpu.VMEM((QCOLS, (MAXA + 1) * BLOCK), BF16),
+            pltpu.VMEM((QCOLS, HDIM), F32),
             pltpu.VMEM((8, 128), jnp.int32),
             pltpu.SMEM((2, 8, 128), jnp.int32),
             dma((13,)),

time: 150 us -> 140 us (0.933)
  Pallas kernels: 146 us -> 135 us
    pallas_call x1, Pallas kernels: 146 us -> 135 us  [on_device(): pl.pallas_call(kernel, out_shape=jax.ShapeDtypeStruct((BLOCK, D), BF16),...]
where the time goes in v4:
time: 140 us; the launch traced here: 139 us
  Pallas kernels  135 us (96%)
  local copies, waits for them, and re-layouts  3.81 us (3%)
    pallas_call x1, Pallas kernels, on_device(): pl.pallas_call(kernel, out_shape=jax.ShapeDtypeStruct((BLOCK, D), BF16),...  135 us
    unnamed x2, local copies, waits for them, and re-layouts  3.21 us

profile of v4, /device:TPU:104, one launch (start us, length us, event | category | flops | bytes accessed | tf_op | source)
XLA Modules:
  0.0 138.6 jit_solution(15012088036574550817)
XLA Ops:
  0.0 0.8 copy.12
  0.8 0.6 pad.4.anc_h
  1.4 134.7 %shard_map.109 = bf16[128,5120]{1,0:T(8,128)(2,1)} custom-call(bf16[128,5120]{1,0:T(8,128)(2,1)} %hid.1, f32[1,5120]{1,0:T(1,128)} %bitcast.1, bf16[5120,640]{1,0:T(8,128)(2,1)} %wq_h.1, bf16[5120,128]{1,0:T(8,128)(2,1)} %wk_h.1, bf16[5120,128]{1,0:T(8,128)(2,1)} %wv_h.1, bf16[640,5120]{1,0:T(8,128)(2,1)} %wo_h.1, s32[8,128]{1,0:T(8,128)} %pad.4.anc_h, ...), custom_call_target="tpu_custom_call" | custom-call | flops 16999999488 | bytes 20000000 | tf_op jit(solution)/shard_map/pallas_call | solution.py:557
  136.1 2.5 %copy.14 = bf16[128,5120]{1,0:T(8,128)(2,1)} copy(bf16[128,5120]{1,0:T(8,128)(2,1)} %shard_map.109) | data formatting | bytes 2621440

commit v5 on v4

--- a/solution.py
+++ b/solution.py
@@ -298,6 +298,7 @@
     wait_weights((0, 1), (0, 1))
     ag(4).wait_recv()
     project_kv(0)
+    start_kv(0)
     ag(1).wait_recv()
     ag(8).start()
     ag(3).wait_recv()
@@ -309,7 +310,7 @@
     def _(i):
         project_kv(1 + 2 * i)
 
-    for r in (0, 1, 3):
+    for r in (1, 3):
         start_kv(r)
     pass_weights((4,))
     wait_weights((2, 3), (2,))
@@ -457,11 +458,14 @@
 
     def open_half(j, attend):
         put_out(2, j)
-        attend(3)
+        if j:
+            put_out(3, j)
         take_sibling(2, j)
         for side in range(2):
             far_send(side, j).start()
-        put_out(3, j)
+        if not j:
+            attend(3)
+            put_out(3, j)
         attend(1)
         put_out(1, j)
         take_sibling(3, j)
@@ -496,8 +500,8 @@
     close_half(0)
     wait_weights((5,), ())
     open_half(1, lambda r: None)
+    close_half(1)
     finish(0)
-    close_half(1)
     finish(1)
 
     for r in range(4):

time: 140 us -> 140 us (level)
  no operation moved by 1% of the time
where the time goes in v5:
time: 140 us; the launch traced here: 138 us
  Pallas kernels  134 us (96%)
  local copies, waits for them, and re-layouts  3.81 us (3%)
    pallas_call x1, Pallas kernels, on_device(): pl.pallas_call(kernel, out_shape=jax.ShapeDtypeStruct((BLOCK, D), BF16),...  134 us
    unnamed x2, local copies, waits for them, and re-layouts  3.21 us

profile of v5, /device:TPU:104, one launch (start us, length us, event | category | flops | bytes accessed | tf_op | source)
XLA Modules:
  0.0 138.2 jit_solution(17603672449369268545)
XLA Ops:
  0.0 0.8 copy.12
  0.8 0.6 pad.4.anc_h
  1.4 134.4 %shard_map.109 = bf16[128,5120]{1,0:T(8,128)(2,1)} custom-call(bf16[128,5120]{1,0:T(8,128)(2,1)} %hid.1, f32[1,5120]{1,0:T(1,128)} %bitcast.1, bf16[5120,640]{1,0:T(8,128)(2,1)} %wq_h.1, bf16[5120,128]{1,0:T(8,128)(2,1)} %wk_h.1, bf16[5120,128]{1,0:T(8,128)(2,1)} %wv_h.1, bf16[640,5120]{1,0:T(8,128)(2,1)} %wo_h.1, s32[8,128]{1,0:T(8,128)} %pad.4.anc_h, ...), custom_call_target="tpu_custom_call" | custom-call | flops 16999999488 | bytes 20000000 | tf_op jit(solution)/shard_map/pallas_call | solution.py:561
  135.8 2.5 %copy.14 = bf16[128,5120]{1,0:T(8,128)(2,1)} copy(bf16[128,5120]{1,0:T(8,128)(2,1)} %shard_map.109) | data formatting | bytes 2621440
